TPU v7x, 32 devices: a whole 2x2x4 slice. The times are simulated.
32 devices in a mesh: dp: 1, gx: 4 (over y, x), gy: 8 (over z, core).
Axes of the slice: x: 2, y: 2, z: 4, core: 2. Of those that a mesh axis runs over, the one named last changes fastest.
Arguments:
- fields: float32 [1, 20, 16, 16, 512], P('dp', None, 'gx', 'gy'), may hold values from -6 to 6
- cotangent: float32 [1, 20, 16, 16, 512], P('dp', None, 'gx', 'gy'), may hold values from -6 to 6
- spectral: float32 [2, 144, 8, 12, 20, 20], P(None, 'gx', 'gy'), may hold values from -6 to 6
- bypass: float32 [20, 20], replicated, may hold values from -1.25 to 1.25
Outputs:
- outputs: float32 [1, 20, 16, 16, 512], P('dp', None, 'gx', 'gy')
- field_grad: float32 [1, 20, 16, 16, 512], P('dp', None, 'gx', 'gy')
- spectral_grad: float32 [2, 144, 8, 12, 20, 20], P(None, 'gx', 'gy')
All inputs are finite; a program needn't handle non-finite values.
Results may differ from a plain program's by a relative error of at most 0.00011.
Values sent between devices are 32-bit elements; how exact they have to be, the bound alone decides.
A program may use at most 64 MiB of HBM per device.

v0:
```python
import functools
import math

import jax
import jax.numpy as jnp
import numpy as np
from jax import lax
from jax.experimental import pallas as pl
from jax.experimental.pallas import tpu as pltpu
from jax.sharding import PartitionSpec as P

STEPS = 8
MODES_X = 12
MODES_Y = 12
MODES_Z = 12
MODES_T = 8
LANES = 128
MESH = pl.DeviceIdType.MESH
close = lax.Precision.HIGH
NN = (((1,), (0,)), ((), ()))
NT = (((1,), (1,)), ((), ()))
TN = (((0,), (0,)), ((), ()))


def up(value, step):
    return -(-value // step) * step


def product(left, right, dims):
    return lax.dot_general(left, right, dims, precision=close, preferred_element_type=jnp.float32)


def signed(amount):
    ids = np.arange(amount)
    return np.where(ids < amount // 2, ids, ids - amount)


class Sizes:
    def __init__(self, sample, spectral, size_x, size_y):
        _, self.chan, self.rows_x, self.rows_y, self.cells = sample
        self.nx, self.ny = size_x, size_y
        self.full_x, self.full_y = self.rows_x * size_x, self.rows_y * size_y
        self.count = self.full_x * self.full_y * self.cells
        self.tiles = self.cells // LANES
        self.qb = spectral[1]
        self.kx = spectral[3]
        self.mb = MODES_Z * MODES_T // size_y
        self.ly = MODES_Y
        self.mb2 = up(2 * self.mb, 8)
        self.half = self.mb2 // 2
        self.cx = self.chan * self.rows_x
        self.cp = up(self.cx, LANES)
        self.kp = up(self.kx, 8)
        self.qbp = up(self.qb, 8)
        self.spec_rows = 2 * self.chan * self.kp

    def pieces(self, mode):
        start, stop, found = mode * self.mb, (mode + 1) * self.mb, []
        while start < stop:
            owner = start // self.qb
            rows = min(stop, (owner + 1) * self.qb) - start
            found.append((owner, start - owner * self.qb, start - mode * self.mb, rows))
            start += rows
        return found


def depth_table(z):
    depth = z.cells // STEPS
    modes = np.arange(MODES_Z * MODES_T)
    freq_z, freq_t = signed(MODES_Z)[modes // MODES_T], signed(MODES_T)[modes % MODES_T]
    cell = np.arange(z.cells)
    turns = freq_z[:, None] * (cell // STEPS) * STEPS + freq_t[:, None] * (cell % STEPS) * depth
    angle = (turns % z.cells) * (2.0 * math.pi / z.cells)
    table = np.zeros((z.ny, 2, z.half, z.cells))
    table[:, 0, : z.mb] = np.cos(angle).reshape(z.ny, z.mb, z.cells)
    table[:, 1, : z.mb] = -np.sin(angle).reshape(z.ny, z.mb, z.cells)
    return table.reshape(z.ny * z.mb2, z.cells).astype(np.float32)


def x_table(z):
    angle = (signed(z.kx)[:, None] * np.arange(z.full_x) % z.full_x) * (2.0 * math.pi / z.full_x)
    cosine = np.cos(angle).reshape(z.kx, z.nx, z.rows_x)
    sine = np.sin(angle).reshape(z.kx, z.nx, z.rows_x)
    table = np.zeros((2, z.chan, z.kp, z.nx, 2, z.cp))
    for c in range(z.chan):
        cols = slice(c * z.rows_x, (c + 1) * z.rows_x)
        table[0, c, : z.kx, :, 0, cols] = cosine
        table[0, c, : z.kx, :, 1, cols] = sine
        table[1, c, : z.kx, :, 0, cols] = -sine
        table[1, c, : z.kx, :, 1, cols] = cosine
    return table.reshape(z.spec_rows, z.nx * 2 * z.cp).astype(np.float32)


def chain(
    z, fields_hbm, cotangent_hbm, depth_hbm, bypass_hbm, spread_hbm, same_hbm, w_hbm, x_hbm,
    output_hbm, grad_hbm, spec_hbm, dual_hbm,
    output, field_grad, spec, dual, fields, cotangent, depth, bypass, spread, same_x, w, xt, unit, mixed, signal, direct, sg, rg, sx, rx, gs, gr, xs, xr, load_sems, store_sems,
):
    me_x, me_y = lax.axis_index("gx"), lax.axis_index("gy")
    axes = {"gx": (me_x, z.nx), "gy": (me_y, z.ny)}

    barrier = pltpu.get_barrier_semaphore()
    for axis, (me, n) in axes.items():
        for step in range(1, n):
            pl.semaphore_signal(
                barrier, inc=1, device_id={axis: lax.rem(me + step, n)}, device_id_type=MESH
            )
    loads = {}
    for name, src, dst in (
        ("depth", depth_hbm, depth),
        ("fields", fields_hbm, fields),
        ("bypass", bypass_hbm, bypass),
        ("spread", spread_hbm, spread),
        ("same_x", same_hbm, same_x),
        ("x", x_hbm, xt),
        ("w", w_hbm, w),
        ("cotangent", cotangent_hbm, cotangent),
    ):
        loads[name] = pltpu.make_async_copy(src, dst, load_sems.at[len(loads)])
        loads[name].start()

    stores = []

    def store(src, dst):
        stores.append(pltpu.make_async_copy(src, dst, store_sems.at[len(stores)]))
        stores[-1].start()

    def send(axis, src, dst, send_sem, recv_sem):
        me, n = axes[axis]
        copies = []
        for step in range(1, n):
            peer = lax.rem(me + step, n)
            copy = pltpu.make_async_remote_copy(
                src_ref=src.at[peer],
                dst_ref=dst.at[me],
                send_sem=send_sem.at[step],
                recv_sem=recv_sem.at[step],
                device_id={axis: peer},
                device_id_type=MESH,
            )
            copy.start()
            copies.append(copy)
        dst[me] = src[me]
        return copies

    def send_y(turn):
        return send("gy", sg.at[turn], rg.at[turn], gs.at[turn], gr.at[turn])

    def send_x(turn):
        return send("gx", sx.at[turn], rx.at[turn], xs.at[turn], xr.at[turn])

    def finish(copies):
        for copy in copies:
            copy.wait()

    stride = z.tiles * z.rows_y

    def cells_of(ref, y):
        parts = [ref[pl.ds(t * z.rows_y + y, z.cx, stride=stride), :] for t in range(z.tiles)]
        return jnp.concatenate(parts, axis=1)

    def put_cells(ref, y, value):
        for t in range(z.tiles):
            ref[pl.ds(t * z.rows_y + y, z.cx, stride=stride), :] = value[:, t * LANES : (t + 1) * LANES]

    def lanes(y):
        return slice((y % z.rows_y) * z.cp, (y % z.rows_y + 1) * z.cp)

    def depth_in(turn, y, cells):
        if z.cp > z.cx:
            cells = jnp.concatenate([cells, jnp.zeros((z.cp - z.cx, z.cells), jnp.float32)], axis=0)
        found = product(depth[...], cells, NT)
        for block in range(z.ny):
            sg[turn, block, :, lanes(y)] = found[block * z.mb2 : (block + 1) * z.mb2]

    def depth_out(turn, y):
        held = rg[turn, :, :, lanes(y)].reshape(z.ny * z.mb2, z.cp)
        return product(held, depth[...], TN)[: z.cx]

    first_half = lax.broadcasted_iota(jnp.int32, (z.mb2, z.cp), 0) < z.half
    minus_i = jnp.where(first_half, 1.0, -1.0)

    def times_minus_i(value):
        return pltpu.roll(value, z.half, 0) * minus_i

    def wave(y, f):
        angle = 2.0 * math.pi * ((y * f) % z.full_y) / z.full_y
        return math.cos(angle), math.sin(angle)

    def total(terms):
        out = None
        for factor, value in terms:
            if abs(factor) < 1e-12:
                continue
            term = value if factor == 1.0 else value * factor
            out = term if out is None else out + term
        return out

    mid, top = z.full_y // 2, z.ly // 2

    def y_in(turn):
        at = [rg[turn, y // z.rows_y, :, lanes(y)] for y in range(z.full_y)]
        even = [at[y] if y in (0, mid) else at[y] + at[z.full_y - y] for y in range(mid + 1)]
        odd = [None if y in (0, mid) else at[y] - at[z.full_y - y] for y in range(mid)]

        def put(mode, value):
            for part in range(2):
                for owner, there, here, rows in z.pieces(mode):
                    low, base = part * z.half + here, part * z.qbp + there
                    sx[turn, owner, base : base + rows, :] = value[low : low + rows]

        for f in range(top + 1):
            cosines = total([(wave(y, f)[0], even[y]) for y in range(mid + 1)])
            if f == 0:
                put(0, cosines)
                continue
            sines = times_minus_i(total([(wave(y, f)[1], odd[y]) for y in range(1, mid)]))
            if f < top:
                put(f, cosines + sines)
            put(z.ly - f, cosines - sines)

    def y_out(turn):
        for mode in range(z.ly):
            for part in range(2):
                for owner, there, here, rows in z.pieces(mode):
                    low, base = part * z.half + here, part * z.qbp + there
                    unit[mode, low : low + rows, :] = rx[turn, owner, base : base + rows, :]
        even, odd = [unit[0]], [None]
        for f in range(1, top + 1):
            back = unit[z.ly - f]
            ahead = unit[f] if f < top else None
            even.append(back if ahead is None else ahead + back)
            odd.append(times_minus_i(back if ahead is None else back - ahead))
        for y in range(mid + 1):
            cosines = total([(wave(y, f)[0], even[f]) for f in range(top + 1)])
            sines = total([(wave(y, f)[1], odd[f]) for f in range(1, top + 1)]) if 0 < y < mid else None
            if sines is None:
                sg[turn, y // z.rows_y, :, lanes(y)] = cosines
                continue
            other = z.full_y - y
            sg[turn, y // z.rows_y, :, lanes(y)] = cosines + sines
            sg[turn, other // z.rows_y, :, lanes(other)] = cosines - sines

    def x_in(turn):
        held = [
            rx[turn, s, part * z.qbp : part * z.qbp + z.qb, :]
            for s in range(z.nx)
            for part in range(2)
        ]
        return product(xt[...], jnp.concatenate(held, axis=1), NT)

    def x_out(turn):
        found = product(mixed[...], xt[...], TN)
        for s in range(z.nx):
            for part in range(2):
                col = (2 * s + part) * z.cp
                sx[turn, s, part * z.qbp : part * z.qbp + z.qb, :] = found[:, col : col + z.cp]

    pairs = z.chan * z.chan

    def mix(source, adjoint, scale):
        def weight(part, kx, channel):
            return w[pl.ds((part * z.kx + kx) * pairs + channel * z.chan, z.chan), :]

        def forward(kx, carry):
            real = jnp.zeros((z.chan, z.qb), jnp.float32)
            imag = jnp.zeros((z.chan, z.qb), jnp.float32)
            for c in range(z.chan):
                w_real, w_imag = weight(0, kx, c), weight(1, kx, c)
                s_real = source[pl.ds(c * z.kp + kx, 1), :]
                s_imag = source[pl.ds((z.chan + c) * z.kp + kx, 1), :]
                real = real + s_real * w_real - s_imag * w_imag
                imag = imag + s_imag * w_real + s_real * w_imag
            mixed[pl.ds(kx, z.chan, stride=z.kp), :] = real * scale
            mixed[pl.ds(z.chan * z.kp + kx, z.chan, stride=z.kp), :] = imag * scale
            return carry

        def backward(kx, carry):
            real = source[pl.ds(kx, z.chan, stride=z.kp), :]
            imag = source[pl.ds(z.chan * z.kp + kx, z.chan, stride=z.kp), :]
            for c in range(z.chan):
                w_real, w_imag = weight(0, kx, c), weight(1, kx, c)
                b_real = jnp.sum(w_real * real + w_imag * imag, axis=0, keepdims=True)
                b_imag = jnp.sum(w_real * imag - w_imag * real, axis=0, keepdims=True)
                mixed[pl.ds(c * z.kp + kx, 1), :] = b_real
                mixed[pl.ds((z.chan + c) * z.kp + kx, 1), :] = b_imag
            return carry

        lax.fori_loop(0, z.kx, backward if adjoint else forward, 0)

    loads["depth"].wait()
    loads["fields"].wait()
    for y in range(z.rows_y):
        depth_in(0, y, cells_of(fields, y))
    pl.semaphore_wait(barrier, z.nx + z.ny - 2)
    moving = send_y(0)
    mixed[...] = jnp.zeros_like(mixed)
    if z.half != z.mb:
        unit[...] = jnp.zeros_like(unit)
    for name in ("bypass", "spread", "same_x"):
        loads[name].wait()
    exact = lax.Precision.HIGHEST
    wide = lax.dot_general(spread[...], bypass[...], NN, precision=exact)
    square = lax.dot_general(wide, spread[...], NT, precision=exact) * same_x[...]
    for y in range(z.rows_y):
        direct[y] = product(square, cells_of(fields, y), TN)
    finish(moving)
    y_in(0)
    moving = send_x(0)
    loads["x"].wait()
    finish(moving)
    spec[...] = x_in(0)
    loads["w"].wait()
    mix(spec, False, 1.0 / z.count)
    x_out(1)
    finish(send_x(1))
    y_out(1)
    finish(send_y(1))
    loads["cotangent"].wait()

    root = math.sqrt(2.0 / math.pi)
    for y in range(z.rows_y):
        pre = depth_out(1, y) + direct[y]
        square_pre = pre * pre
        bend = jnp.tanh(root * (pre + 0.044715 * (square_pre * pre)))
        put_cells(output, y, 0.5 * pre * (1.0 + bend))
        slope = 0.5 * (1.0 + bend) + 0.5 * pre * (1.0 - bend * bend) * (
            root * (1.0 + 3.0 * 0.044715 * square_pre)
        )
        back = cells_of(cotangent, y) * slope
        signal[y] = back
        depth_in(2, y, back)

    moving = send_y(2)
    store(spec, spec_hbm)
    store(output, output_hbm)
    for y in range(z.rows_y):
        direct[y] = product(square, signal[y], NN)
    finish(moving)
    y_in(2)
    finish(send_x(2))
    dual[...] = x_in(2) * (1.0 / z.count)
    mix(dual, True, None)
    x_out(3)
    moving = send_x(3)
    store(dual, dual_hbm)
    finish(moving)
    y_out(3)
    finish(send_y(3))
    for y in range(z.rows_y):
        put_cells(field_grad, y, depth_out(3, y) + direct[y])
    store(field_grad, grad_hbm)
    finish(stores)


def outer(z, spec, dual, first, second, grad_hbm, first_out, second_out, grad, sems):
    pairs = z.chan * z.chan
    per_part = z.kx * pairs
    moves = [
        pltpu.make_async_copy(first, first_out, sems.at[0]),
        pltpu.make_async_copy(second, second_out, sems.at[1]),
    ]
    for move in moves:
        move.start()
    for part in range(2):
        sign = 1.0 - 2.0 * part

        def body(kx, carry):
            same = dual[pl.ds(part * z.chan * z.kp + kx, z.chan, stride=z.kp), :]
            cross = dual[pl.ds((1 - part) * z.chan * z.kp + kx, z.chan, stride=z.kp), :] * sign
            for c in range(z.chan):
                real = spec[pl.ds(c * z.kp + kx, 1), :]
                imag = spec[pl.ds((z.chan + c) * z.kp + kx, 1), :]
                at = part * per_part + kx * pairs + c * z.chan
                grad[pl.ds(at, z.chan), : z.qb] = real * same + imag * cross
            return carry

        lax.fori_loop(0, z.kx, body, 0)
        rows = pl.ds(part * per_part, per_part)
        move = pltpu.make_async_copy(grad.at[rows], grad_hbm.at[rows], sems.at[2 + part])
        move.start()
        moves.append(move)
    for move in moves:
        move.wait()


def on_device(fields, cotangent, spectral, bypass):
    z = Sizes(fields.shape, spectral.shape, lax.axis_size("gx"), lax.axis_size("gy"))
    f32 = jnp.float32

    def rows(value):
        shaped = value.reshape(z.chan, z.rows_x, z.rows_y, z.tiles, LANES)
        return shaped.transpose(0, 1, 3, 2, 4).reshape(-1, LANES)

    def unrows(value):
        shaped = value.reshape(z.chan, z.rows_x, z.tiles, z.rows_y, LANES)
        return shaped.transpose(0, 1, 3, 2, 4).reshape(fields.shape)

    weights = spectral.transpose(0, 3, 4, 5, 2, 1).reshape(-1, z.qb)
    wide = (weights.shape[0], up(z.qb, LANES))
    spread = np.kron(np.eye(z.chan), np.ones((z.rows_x, 1))).astype(np.float32)
    same_x = np.kron(np.ones((z.chan, z.chan)), np.eye(z.rows_x)).astype(np.float32)
    x_cols = z.nx * 2 * z.cp
    vmem = pl.BlockSpec(memory_space=pltpu.VMEM)
    hbm = pl.BlockSpec(memory_space=pltpu.HBM)
    any_space = pl.BlockSpec(memory_space=pl.ANY)
    grid_rows = z.cx * z.rows_y * z.tiles
    y_block = (4, z.ny, z.mb2, z.rows_y * z.cp)
    x_block = (4, z.nx, 2 * z.qbp, z.cp)
    output, field_grad, spec, dual = pl.pallas_call(
        functools.partial(chain, z),
        out_shape=(
            jax.ShapeDtypeStruct((grid_rows, LANES), f32),
            jax.ShapeDtypeStruct((grid_rows, LANES), f32),
            jax.ShapeDtypeStruct((z.spec_rows, z.qb), f32),
            jax.ShapeDtypeStruct((z.spec_rows, z.qb), f32),
        ),
        in_specs=[hbm] * 8,
        out_specs=[hbm] * 4,
        scratch_shapes=[
            pltpu.VMEM((grid_rows, LANES), f32),
            pltpu.VMEM((grid_rows, LANES), f32),
            pltpu.VMEM((z.spec_rows, z.qb), f32),
            pltpu.VMEM((z.spec_rows, z.qb), f32),
            pltpu.VMEM((grid_rows, LANES), f32),
            pltpu.VMEM((grid_rows, LANES), f32),
            pltpu.VMEM((z.ny * z.mb2, z.cells), f32),
            pltpu.VMEM(bypass.shape, f32),
            pltpu.VMEM(spread.shape, f32),
            pltpu.VMEM(same_x.shape, f32),
            pltpu.VMEM(weights.shape, f32),
            pltpu.VMEM((z.spec_rows, x_cols), f32),
            pltpu.VMEM((z.ly, z.mb2, z.cp), f32),
            pltpu.VMEM((z.spec_rows, z.qb), f32),
            pltpu.VMEM((z.rows_y, z.cx, z.cells), f32),
            pltpu.VMEM((z.rows_y, z.cx, z.cells), f32),
            pltpu.VMEM(y_block, f32),
            pltpu.VMEM(y_block, f32),
            pltpu.VMEM(x_block, f32),
            pltpu.VMEM(x_block, f32),
            pltpu.SemaphoreType.DMA((4, z.ny)),
            pltpu.SemaphoreType.DMA((4, z.ny)),
            pltpu.SemaphoreType.DMA((4, z.nx)),
            pltpu.SemaphoreType.DMA((4, z.nx)),
            pltpu.SemaphoreType.DMA((8,)),
            pltpu.SemaphoreType.DMA((4,)),
        ],
        compiler_params=pltpu.CompilerParams(
            collective_id=0, has_side_effects=True, vmem_limit_bytes=61 << 20
        ),
        name="fourier_chain",
    )(
        rows(fields), rows(cotangent), depth_table(z), bypass, spread, same_x, weights, x_table(z)
    )
    local_grad, output, field_grad = pl.pallas_call(
        functools.partial(outer, z),
        out_shape=(
            jax.ShapeDtypeStruct(wide, f32),
            jax.ShapeDtypeStruct((grid_rows, LANES), f32),
            jax.ShapeDtypeStruct((grid_rows, LANES), f32),
        ),
        in_specs=[vmem] * 4,
        out_specs=[any_space] * 3,
        scratch_shapes=[pltpu.VMEM(wide, f32), pltpu.SemaphoreType.DMA((4,))],
        compiler_params=pltpu.CompilerParams(vmem_limit_bytes=61 << 20),
        name="outer_products",
    )(spec, dual, output, field_grad)
    local_grad = lax.optimization_barrier(local_grad[:, : z.qb]).reshape(-1, 1, z.qb)
    local_grad = lax.optimization_barrier(local_grad)
    spectral_grad = local_grad.reshape(2, z.kx, z.chan, z.chan, 1, z.qb).transpose(0, 5, 4, 1, 2, 3)
    if lax.axis_size("dp") > 1:
        spectral_grad = lax.psum(spectral_grad, "dp")
    return (unrows(output), unrows(field_grad), spectral_grad)


def solution(mesh):
    cells = P("dp", None, "gx", "gy", None)
    weights = P(None, "gx", "gy", None, None, None)
    return jax.shard_map(
        on_device,
        mesh=mesh,
        in_specs=(cells, cells, weights, P()),
        out_specs=(cells, cells, weights),
        check_vma=False,
    )
```

profile of v0, /device:TPU:0, one launch (start us, length us, event | category | flops | bytes accessed | tf_op | source)
XLA Modules:
  0.0 58.3 jit_solution(7629170804285786303)
XLA Ops:
  0.6 53.7 %fourier_chain.1 = (f32[640,128]{1,0:T(8,128)}, f32[640,128]{1,0:T(8,128)}, f32[640,36]{1,0:T(8,128)}, f32[640,36]{1,0:T(8,128)}) custom-call(f32[640,128]{1,0:T(8,128)} %bitcast.29, f32[640,128]{1,0:T(8,128)} %bitcast.30, f32[192,512]{1,0:T(8,128)} %constant.8.clone.depth_hbm, f32[20,20]{1,0:T(8,128)} %bypass_hbm.1, f32[80,20]{1,0:T(8,128)} %constant.9.clone.spread_hbm, ...), custom_call_target="tpu_custom_call" | custom-call | tf_op jit(solution)/shard_map/fourier_chain/pallas_call | solution.py:410
  54.3 4.0 %outer_products.1 = (f32[9600,128]{1,0:T(8,128)}, f32[640,128]{1,0:T(8,128)}, f32[640,128]{1,0:T(8,128)}) custom-call(f32[640,36]{1,0:T(8,128)} %get-tuple-element.10.spec, f32[640,36]{1,0:T(8,128)} %get-tuple-element.11.dual, f32[640,128]{1,0:T(8,128)} %get-tuple-element.12.first, f32[640,128]{1,0:T(8,128)} %get-tuple-element.13.second), custom_call_target="tpu_custom_call" | custom-call | tf_op jit(solution)/shard_map/outer_products/pallas_call | solution.py:455
where the time goes:
time: 58.5 us; the launch traced here: 58.3 us
  Pallas kernels  57.7 us (99%)
  between operations  0.64 us (1%)
    pallas_call x1, Pallas kernels, on_device(): pl.pallas_call(functools.partial(chain, z), out_shape=(jax.ShapeDtypeStru...  53.7 us
    pallas_call x1, Pallas kernels, on_device(): pl.pallas_call(functools.partial(outer, z), out_shape=(jax.ShapeDtypeStru...  4.02 us

commit v1 on v0

--- a/solution.py
+++ b/solution.py
@@ -143,8 +143,8 @@
         dst[me] = src[me]
         return copies
 
-    def send_y(turn):
-        return send("gy", sg.at[turn], rg.at[turn], gs.at[turn], gr.at[turn])
+    def send_y(turn, y):
+        return send("gy", sg.at[turn, y], rg.at[turn, y], gs.at[turn, y], gr.at[turn, y])
 
     def send_x(turn):
         return send("gx", sx.at[turn], rx.at[turn], xs.at[turn], xr.at[turn])
@@ -162,19 +162,16 @@
     def put_cells(ref, y, value):
         for t in range(z.tiles):
             ref[pl.ds(t * z.rows_y + y, z.cx, stride=stride), :] = value[:, t * LANES : (t + 1) * LANES]
-
-    def lanes(y):
-        return slice((y % z.rows_y) * z.cp, (y % z.rows_y + 1) * z.cp)
 
     def depth_in(turn, y, cells):
         if z.cp > z.cx:
             cells = jnp.concatenate([cells, jnp.zeros((z.cp - z.cx, z.cells), jnp.float32)], axis=0)
         found = product(depth[...], cells, NT)
         for block in range(z.ny):
-            sg[turn, block, :, lanes(y)] = found[block * z.mb2 : (block + 1) * z.mb2]
+            sg[turn, y, block] = found[block * z.mb2 : (block + 1) * z.mb2]
 
     def depth_out(turn, y):
-        held = rg[turn, :, :, lanes(y)].reshape(z.ny * z.mb2, z.cp)
+        held = rg[turn, y].reshape(z.ny * z.mb2, z.cp)
         return product(held, depth[...], TN)[: z.cx]
 
     first_half = lax.broadcasted_iota(jnp.int32, (z.mb2, z.cp), 0) < z.half
@@ -199,7 +196,7 @@
     mid, top = z.full_y // 2, z.ly // 2
 
     def y_in(turn):
-        at = [rg[turn, y // z.rows_y, :, lanes(y)] for y in range(z.full_y)]
+        at = [rg[turn, y % z.rows_y, y // z.rows_y] for y in range(z.full_y)]
         even = [at[y] if y in (0, mid) else at[y] + at[z.full_y - y] for y in range(mid + 1)]
         odd = [None if y in (0, mid) else at[y] - at[z.full_y - y] for y in range(mid)]
 
@@ -231,15 +228,24 @@
             ahead = unit[f] if f < top else None
             even.append(back if ahead is None else ahead + back)
             odd.append(times_minus_i(back if ahead is None else back - ahead))
-        for y in range(mid + 1):
+        made, copies = set(), {}
+
+        def put(y, value):
+            sg[turn, y % z.rows_y, y // z.rows_y] = value
+            made.add(y)
+
+        for y in sorted(range(mid + 1), key=lambda y: y % z.rows_y):
             cosines = total([(wave(y, f)[0], even[f]) for f in range(top + 1)])
-            sines = total([(wave(y, f)[1], odd[f]) for f in range(1, top + 1)]) if 0 < y < mid else None
-            if sines is None:
-                sg[turn, y // z.rows_y, :, lanes(y)] = cosines
-                continue
-            other = z.full_y - y
-            sg[turn, y // z.rows_y, :, lanes(y)] = cosines + sines
-            sg[turn, other // z.rows_y, :, lanes(other)] = cosines - sines
+            if y in (0, mid):
+                put(y, cosines)
+            else:
+                sines = total([(wave(y, f)[1], odd[f]) for f in range(1, top + 1)])
+                put(y, cosines + sines)
+                put(z.full_y - y, cosines - sines)
+            for row in range(z.rows_y):
+                if row not in copies and made.issuperset(range(row, z.full_y, z.rows_y)):
+                    copies[row] = send_y(turn, row)
+        return copies
 
     def x_in(turn):
         held = [
@@ -288,12 +294,14 @@
 
         lax.fori_loop(0, z.kx, backward if adjoint else forward, 0)
 
+    moving = []
     loads["depth"].wait()
     loads["fields"].wait()
     for y in range(z.rows_y):
         depth_in(0, y, cells_of(fields, y))
-    pl.semaphore_wait(barrier, z.nx + z.ny - 2)
-    moving = send_y(0)
+        if y == 0:
+            pl.semaphore_wait(barrier, z.nx + z.ny - 2)
+        moving += send_y(0, y)
     mixed[...] = jnp.zeros_like(mixed)
     if z.half != z.mb:
         unit[...] = jnp.zeros_like(unit)
@@ -314,12 +322,13 @@
     mix(spec, False, 1.0 / z.count)
     x_out(1)
     finish(send_x(1))
-    y_out(1)
-    finish(send_y(1))
+    arriving = y_out(1)
     loads["cotangent"].wait()
 
     root = math.sqrt(2.0 / math.pi)
+    moving = []
     for y in range(z.rows_y):
+        finish(arriving[y])
         pre = depth_out(1, y) + direct[y]
         square_pre = pre * pre
         bend = jnp.tanh(root * (pre + 0.044715 * (square_pre * pre)))
@@ -330,8 +339,8 @@
         back = cells_of(cotangent, y) * slope
         signal[y] = back
         depth_in(2, y, back)
-
-    moving = send_y(2)
+        moving += send_y(2, y)
+
     store(spec, spec_hbm)
     store(output, output_hbm)
     for y in range(z.rows_y):
@@ -345,9 +354,9 @@
     moving = send_x(3)
     store(dual, dual_hbm)
     finish(moving)
-    y_out(3)
-    finish(send_y(3))
+    arriving = y_out(3)
     for y in range(z.rows_y):
+        finish(arriving[y])
         put_cells(field_grad, y, depth_out(3, y) + direct[y])
     store(field_grad, grad_hbm)
     finish(stores)
@@ -405,7 +414,7 @@
     hbm = pl.BlockSpec(memory_space=pltpu.HBM)
     any_space = pl.BlockSpec(memory_space=pl.ANY)
     grid_rows = z.cx * z.rows_y * z.tiles
-    y_block = (4, z.ny, z.mb2, z.rows_y * z.cp)
+    y_block = (4, z.rows_y, z.ny, z.mb2, z.cp)
     x_block = (4, z.nx, 2 * z.qbp, z.cp)
     output, field_grad, spec, dual = pl.pallas_call(
         functools.partial(chain, z),
@@ -438,8 +447,8 @@
             pltpu.VMEM(y_block, f32),
             pltpu.VMEM(x_block, f32),
             pltpu.VMEM(x_block, f32),
-            pltpu.SemaphoreType.DMA((4, z.ny)),
-            pltpu.SemaphoreType.DMA((4, z.ny)),
+            pltpu.SemaphoreType.DMA((4, z.rows_y, z.ny)),
+            pltpu.SemaphoreType.DMA((4, z.rows_y, z.ny)),
             pltpu.SemaphoreType.DMA((4, z.nx)),
             pltpu.SemaphoreType.DMA((4, z.nx)),
             pltpu.SemaphoreType.DMA((8,)),

time: 58.5 us -> 58.8 us (level)
  no operation moved by 1% of the time
where the time goes in v1:
time: 58.8 us; the launch traced here: 58.6 us
  Pallas kernels  58 us (99%)
  between operations  0.64 us (1%)
    pallas_call x1, Pallas kernels, on_device(): pl.pallas_call(functools.partial(chain, z), out_shape=(jax.ShapeDtypeStru...  54 us
    pallas_call x1, Pallas kernels, on_device(): pl.pallas_call(functools.partial(outer, z), out_shape=(jax.ShapeDtypeStru...  4.02 us

profile of v1, /device:TPU:0, one launch (start us, length us, event | category | flops | bytes accessed | tf_op | source)
XLA Modules:
  0.0 58.6 jit_solution(7963516894659827967)
XLA Ops:
  0.6 54.0 %fourier_chain.1 = (f32[640,128]{1,0:T(8,128)}, f32[640,128]{1,0:T(8,128)}, f32[640,36]{1,0:T(8,128)}, f32[640,36]{1,0:T(8,128)}) custom-call(f32[640,128]{1,0:T(8,128)} %bitcast.29, f32[640,128]{1,0:T(8,128)} %bitcast.30, f32[192,512]{1,0:T(8,128)} %constant.8.clone.depth_hbm, f32[20,20]{1,0:T(8,128)} %bypass_hbm.1, f32[80,20]{1,0:T(8,128)} %constant.9.clone.spread_hbm, ...), custom_call_target="tpu_custom_call" | custom-call | tf_op jit(solution)/shard_map/fourier_chain/pallas_call | solution.py:419
  54.6 4.0 %outer_products.1 = (f32[9600,128]{1,0:T(8,128)}, f32[640,128]{1,0:T(8,128)}, f32[640,128]{1,0:T(8,128)}) custom-call(f32[640,36]{1,0:T(8,128)} %get-tuple-element.10.spec, f32[640,36]{1,0:T(8,128)} %get-tuple-element.11.dual, f32[640,128]{1,0:T(8,128)} %get-tuple-element.12.first, f32[640,128]{1,0:T(8,128)} %get-tuple-element.13.second), custom_call_target="tpu_custom_call" | custom-call | tf_op jit(solution)/shard_map/outer_products/pallas_call | solution.py:464

commit v2 on v1

--- a/solution.py
+++ b/solution.py
@@ -164,17 +164,15 @@
             ref[pl.ds(t * z.rows_y + y, z.cx, stride=stride), :] = value[:, t * LANES : (t + 1) * LANES]
 
     def depth_in(turn, y, cells):
-        if z.cp > z.cx:
-            cells = jnp.concatenate([cells, jnp.zeros((z.cp - z.cx, z.cells), jnp.float32)], axis=0)
         found = product(depth[...], cells, NT)
         for block in range(z.ny):
             sg[turn, y, block] = found[block * z.mb2 : (block + 1) * z.mb2]
 
     def depth_out(turn, y):
-        held = rg[turn, y].reshape(z.ny * z.mb2, z.cp)
-        return product(held, depth[...], TN)[: z.cx]
-
-    first_half = lax.broadcasted_iota(jnp.int32, (z.mb2, z.cp), 0) < z.half
+        held = rg[turn, y].reshape(z.ny * z.mb2, z.cx)
+        return product(held, depth[...], TN)
+
+    first_half = lax.broadcasted_iota(jnp.int32, (z.mb2, z.cx), 0) < z.half
     minus_i = jnp.where(first_half, 1.0, -1.0)
 
     def times_minus_i(value):
@@ -253,6 +251,9 @@
             for s in range(z.nx)
             for part in range(2)
         ]
+        if z.cp > z.cx:
+            blank = jnp.zeros((z.qb, z.cp - z.cx), jnp.float32)
+            held = [jnp.concatenate([block, blank], axis=1) for block in held]
         return product(xt[...], jnp.concatenate(held, axis=1), NT)
 
     def x_out(turn):
@@ -260,7 +261,7 @@
         for s in range(z.nx):
             for part in range(2):
                 col = (2 * s + part) * z.cp
-                sx[turn, s, part * z.qbp : part * z.qbp + z.qb, :] = found[:, col : col + z.cp]
+                sx[turn, s, part * z.qbp : part * z.qbp + z.qb, :] = found[:, col : col + z.cx]
 
     pairs = z.chan * z.chan
 
@@ -414,8 +415,8 @@
     hbm = pl.BlockSpec(memory_space=pltpu.HBM)
     any_space = pl.BlockSpec(memory_space=pl.ANY)
     grid_rows = z.cx * z.rows_y * z.tiles
-    y_block = (4, z.rows_y, z.ny, z.mb2, z.cp)
-    x_block = (4, z.nx, 2 * z.qbp, z.cp)
+    y_block = (4, z.rows_y, z.ny, z.mb2, z.cx)
+    x_block = (4, z.nx, 2 * z.qbp, z.cx)
     output, field_grad, spec, dual = pl.pallas_call(
         functools.partial(chain, z),
         out_shape=(
@@ -439,7 +440,7 @@
             pltpu.VMEM(same_x.shape, f32),
             pltpu.VMEM(weights.shape, f32),
             pltpu.VMEM((z.spec_rows, x_cols), f32),
-            pltpu.VMEM((z.ly, z.mb2, z.cp), f32),
+            pltpu.VMEM((z.ly, z.mb2, z.cx), f32),
             pltpu.VMEM((z.spec_rows, z.qb), f32),
             pltpu.VMEM((z.rows_y, z.cx, z.cells), f32),
             pltpu.VMEM((z.rows_y, z.cx, z.cells), f32),

time: 58.8 us -> 58.8 us (level)
  no operation moved by 1% of the time
where the time goes in v2:
time: 58.8 us; the launch traced here: 58.6 us
  Pallas kernels  58 us (99%)
  between operations  0.64 us (1%)
    pallas_call x1, Pallas kernels, on_device(): pl.pallas_call(functools.partial(chain, z), out_shape=(jax.ShapeDtypeStru...  54 us
    pallas_call x1, Pallas kernels, on_device(): pl.pallas_call(functools.partial(outer, z), out_shape=(jax.ShapeDtypeStru...  4.02 us

profile of v2, /device:TPU:0, one launch (start us, length us, event | category | flops | bytes accessed | tf_op | source)
XLA Modules:
  0.0 58.6 jit_solution(12948769723136451009)
XLA Ops:
  0.6 54.0 %fourier_chain.1 = (f32[640,128]{1,0:T(8,128)}, f32[640,128]{1,0:T(8,128)}, f32[640,36]{1,0:T(8,128)}, f32[640,36]{1,0:T(8,128)}) custom-call(f32[640,128]{1,0:T(8,128)} %bitcast.29, f32[640,128]{1,0:T(8,128)} %bitcast.30, f32[192,512]{1,0:T(8,128)} %constant.8.clone.depth_hbm, f32[20,20]{1,0:T(8,128)} %bypass_hbm.1, f32[80,20]{1,0:T(8,128)} %constant.9.clone.spread_hbm, ...), custom_call_target="tpu_custom_call" | custom-call | tf_op jit(solution)/shard_map/fourier_chain/pallas_call | solution.py:420
  54.6 4.0 %outer_products.1 = (f32[9600,128]{1,0:T(8,128)}, f32[640,128]{1,0:T(8,128)}, f32[640,128]{1,0:T(8,128)}) custom-call(f32[640,36]{1,0:T(8,128)} %get-tuple-element.10.spec, f32[640,36]{1,0:T(8,128)} %get-tuple-element.11.dual, f32[640,128]{1,0:T(8,128)} %get-tuple-element.12.first, f32[640,128]{1,0:T(8,128)} %get-tuple-element.13.second), custom_call_target="tpu_custom_call" | custom-call | tf_op jit(solution)/shard_map/outer_products/pallas_call | solution.py:465
